TPU v7x, 32 devices: a whole 2x2x4 slice. The times are simulated.
32 devices in a mesh: band: 8 (over z, x), slab: 4 (over y, core).
Axes of the slice: x: 2, y: 2, z: 4, core: 2. Of those that a mesh axis runs over, the one named last changes fastest.
Arguments:
- orbitals: float32 [32, 128, 128, 128], P('band', 'slab'), may hold values from -6 to 6
- owner_band: int32 [4], replicated, may hold values from 0 to 7
- owner_slot: int32 [4], replicated, may hold values from 0 to 3
- g_mask: int32 [128, 128, 128], P(None, 'slab'), may hold values from 0 to 1, as said below
Outputs:
- exchange_action: float32 [32, 128, 128, 128], P('band', 'slab')
Inputs may be any that keep to these rules, and one draw needn't show every extreme that they name: `owner_band`: the band index of the device that holds source orbital j. `owner_slot`: the position of source orbital j among its owner's 4 orbitals. 1 where the kernel is kept and 0 where it is cut; the point of zero wave vector, g_mask[0, 0, 0], is always cut.
All inputs are finite; a program needn't handle non-finite values.
Results may differ from a plain program's by a relative error of at most 0.0003.
Values sent between devices are 32-bit elements; how exact they have to be, the bound alone decides.
A program may use at most 192 MiB of HBM per device.

v0:
```python
import math

import jax
import jax.numpy as jnp
from jax import lax
from jax.sharding import PartitionSpec as P

GRID = 128


coulomb_gain = 128.0 * math.pi


def broadcast(value, axis, source):
    kept = jnp.where(lax.axis_index(axis) == source, value, 0).astype(value.dtype)
    return lax.psum(kept, axis)


def cas_matrix(count):
    wave_index = jnp.arange(count, dtype=jnp.int32)
    products = wave_index[:, None] * wave_index[None, :] % count
    angles = 2.0 * math.pi / count * products.astype(jnp.float32)
    return jnp.cos(angles) + jnp.sin(angles)


def fold_index(wave_index):
    return jnp.where(wave_index < GRID // 2, wave_index, wave_index - GRID).astype(jnp.float32)


def transform_planes(field, cas_rows):
    highest = lax.Precision.HIGHEST
    field = jnp.einsum("oxyz,kz->oxyk", field, cas_rows, precision=highest)
    return jnp.einsum("oxyz,ky->oxkz", field, cas_rows, precision=highest)


def transform_first(field, cas_rows):
    return jnp.einsum("oxyz,kx->okyz", field, cas_rows, precision=lax.Precision.HIGHEST)


def fetch_source(orbitals, owner_band, owner_slot, which):
    local_copy = lax.dynamic_index_in_dim(orbitals, owner_slot[which], 0, keepdims=False)
    return broadcast(local_copy, "band", owner_band[which])


def per_device(orbitals, owner_band, owner_slot, g_mask):
    cas_rows = cas_matrix(GRID)
    columns_dev = g_mask.shape[1]
    full_index = jnp.arange(GRID, dtype=jnp.int32)
    column_index = lax.axis_index("slab") * columns_dev + jnp.arange(columns_dev, dtype=jnp.int32)
    first_sq = fold_index(full_index) ** 2
    second_sq = fold_index(column_index) ** 2
    squares = first_sq[:, None, None] + second_sq[None, :, None] + first_sq[None, None, :]
    coulomb = g_mask.astype(jnp.float32) * coulomb_gain / (squares + 1.0)
    inverse = 1.0 / (GRID * GRID * GRID)
    source_count = owner_band.shape[0]
    sources = jnp.stack(
        [fetch_source(orbitals, owner_band, owner_slot, which) for which in range(source_count)]
    )
    accumulated = jnp.zeros(orbitals.shape, jnp.float32)
    for which in range(source_count):
        source_field = sources[which]
        density = orbitals * source_field[None]
        spectrum = transform_planes(density, cas_rows)
        items = lax.all_to_all(spectrum, "slab", split_axis=2, concat_axis=1, tiled=True)
        weigh_spectrum = transform_first(items, cas_rows) * coulomb[None]
        potential = transform_first(weigh_spectrum, cas_rows)
        potential = lax.all_to_all(potential, "slab", split_axis=1, concat_axis=2, tiled=True)
        potential = transform_planes(potential, cas_rows) * inverse
        accumulated = accumulated - potential * source_field[None]
    return accumulated


def solution(mesh):
    return jax.shard_map(
        per_device,
        mesh=mesh,
        in_specs=(P("band", "slab", None, None), P(), P(), P(None, "slab", None)),
        out_specs=P("band", "slab", None, None),
        check_vma=False,
    )
```

profile of v0, /device:TPU:0, one launch (start us, length us, event | category | flops | bytes accessed | tf_op | source)
XLA Modules:
  0.0 1164.9 jit_solution(12261178417186420591)
XLA Ops:
  27.2 275.4 %all-reduce.3.cloned.1.call-done = (f32[32,128,128]{2,1,0:T(8,128)}, f32[32,128,128]{2,1,0:T(8,128)}, f32[32,128,128]{2,1,0:T(8,128)}, f32[32,128,128]{2,1,0:T(8,128)}) async-done(((f32[32,128,128]{2,1,0:T(8,128)}, f32[32,128,128]{2,1,0:T(8,128)}, f32[32,128,128]{2,1,0:T(8,128)}, f32[32,128,128]{2,1,0:T(8,128)}), (f32[32,128,128]{2,1,0:T(8,128)}, f32[32,128,128]{2,1,0:T(8,128)}, f32[32,128,128]{2,1,0:T(8,128)}, ...) | async-done | bytes 8388624 | tf_op jit(solution)/shard_map/psum | solution.py:16
  302.5 10.5 fusion.30
  336.4 10.0 fusion.27
  363.5 66.1 %all-to-all-done = f32[4,32,128,128]{3,1,0,2:T(8,128)} async-done(((f32[4,32,128,128]{3,1,0,2:T(8,128)}), f32[4,32,128,128]{3,1,0,2:T(8,128)}, u32[]{:S(2)}, u32[]{:S(2)}) %all-to-all-start) | async-done | bytes 8388640 | tf_op jit(solution)/shard_map/all_to_all | solution.py:64
  435.2 10.0 fusion.24
  462.7 65.7 %all-to-all-done.2 = f32[4,32,128,128]{3,1,0,2:T(8,128)} async-done(((f32[4,32,128,128]{3,1,0,2:T(8,128)}), f32[4,32,128,128]{3,1,0,2:T(8,128)}, u32[]{:S(2)}, u32[]{:S(2)}) %all-to-all-start.2) | async-done | bytes 8388640 | tf_op jit(solution)/shard_map/all_to_all | solution.py:64
  534.1 10.0 fusion.21
  561.2 66.1 %all-to-all-done.4 = f32[4,32,128,128]{3,1,0,2:T(8,128)} async-done(((f32[4,32,128,128]{3,1,0,2:T(8,128)}), f32[4,32,128,128]{3,1,0,2:T(8,128)}, u32[]{:S(2)}, u32[]{:S(2)}) %all-to-all-start.4) | async-done | bytes 8388640 | tf_op jit(solution)/shard_map/all_to_all | solution.py:64
  644.9 12.7 %fusion.18 = f32[128,4,32,128]{3,0,2,1:T(8,128)S(1)} fusion(f32[4,128,32,128]{3,2,1,0:T(8,128)S(1)} %bitcast.172), kind=kOutput, calls=%fused_computation.22 | convolution fusion | flops 3221471232 | bytes 16777216 | tf_op jit(solution)/shard_map/oxyz,kx->okyz/dot_general | solution.py:37
  675.2 50.9 %all-to-all-done.6 = f32[4,32,128,128]{3,1,0,2:T(8,128)} async-done(((f32[4,32,128,128]{3,1,0,2:T(8,128)}), f32[4,32,128,128]{3,1,0,2:T(8,128)}, u32[]{:S(2)}, u32[]{:S(2)}) %all-to-all-start.6) | async-done | bytes 8388640 | tf_op jit(solution)/shard_map/all_to_all | solution.py:64
  731.9 9.9 copy.38
  741.8 12.6 %fusion.16 = f32[128,4,32,128]{3,0,2,1:T(8,128)S(1)} fusion(f32[4,128,32,128]{3,2,1,0:T(8,128)S(1)} %bitcast.173), kind=kOutput, calls=%fused_computation.20 | convolution fusion | flops 3221471232 | bytes 16777216 | tf_op jit(solution)/shard_map/oxyz,kx->okyz/dot_general | solution.py:37
  771.9 53.0 %all-to-all-done.1 = f32[4,128,32,128]{3,2,0,1:T(8,128)} async-done(((f32[4,128,32,128]{3,2,0,1:T(8,128)}), f32[4,128,32,128]{3,2,0,1:T(8,128)}, u32[]{:S(2)}, u32[]{:S(2)}) %all-to-all-start.1) | async-done | bytes 8388640 | tf_op jit(solution)/shard_map/all_to_all | solution.py:67
  830.8 9.9 copy.45
  840.6 12.6 %fusion.14 = f32[128,4,32,128]{3,0,2,1:T(8,128)S(1)} fusion(f32[4,128,32,128]{3,2,1,0:T(8,128)S(1)} %bitcast.174), kind=kOutput, calls=%fused_computation.18 | convolution fusion | flops 3221471232 | bytes 16777216 | tf_op jit(solution)/shard_map/oxyz,kx->okyz/dot_general | solution.py:37
  870.9 52.8 %all-to-all-done.3 = f32[4,128,32,128]{3,2,0,1:T(8,128)} async-done(((f32[4,128,32,128]{3,2,0,1:T(8,128)}), f32[4,128,32,128]{3,2,0,1:T(8,128)}, u32[]{:S(2)}, u32[]{:S(2)}) %all-to-all-start.3) | async-done | bytes 8388640 | tf_op jit(solution)/shard_map/all_to_all | solution.py:67
  939.4 12.7 %fusion.12 = f32[128,4,32,128]{3,0,2,1:T(8,128)S(1)} fusion(f32[4,128,32,128]{3,2,1,0:T(8,128)S(1)} %bitcast.175), kind=kOutput, calls=%fused_computation.16 | convolution fusion | flops 3221471232 | bytes 16777216 | tf_op jit(solution)/shard_map/oxyz,kx->okyz/dot_general | solution.py:37
  969.6 53.0 %all-to-all-done.5 = f32[4,128,32,128]{3,2,0,1:T(8,128)} async-done(((f32[4,128,32,128]{3,2,0,1:T(8,128)}), f32[4,128,32,128]{3,2,0,1:T(8,128)}, u32[]{:S(2)}, u32[]{:S(2)}) %all-to-all-start.5) | async-done | bytes 8388640 | tf_op jit(solution)/shard_map/all_to_all | solution.py:67
  1051.8 10.2 fusion.80
  1062.0 10.0 fusion.78
  1080.9 10.1 fusion.70
  1099.6 10.3 fusion.62
  1109.9 11.6 all-to-all-done.7
  1135.3 22.2 %fusion = f32[4,32,128,128]{3,2,1,0:T(8,128)} fusion(f32[128,4,32,128]{3,0,2,1:T(8,128)} %fusion.62, f32[128,4,32,128]{3,0,2,1:T(8,128)} %fusion.70, f32[128,4,32,128]{3,0,2,1:T(8,128)} %fusion.78, f32[32,128,128]{2,1,0:T(8,128)S(1)} %copy-done.6, f32[32,128,128]{2,1,0:T(8,128)} %get-tuple-element.22, f32[32,128,128]{2,1,0:T(8,128)} %get-tuple-element.23, ...), kind=kOutput, calls=%fused_computation.1 | convolution fusion | flops 3238248448 | bytes 50331648 | tf_op jit(solution)/shard_map/oxyz,ky->oxkz/dot_general | solution.py:33
  (61 shorter events, 272.2 us)
Async XLA Ops:
  6.5 296.0 %all-reduce.3.cloned.1.call-start = ((), (), s32[]{:S(2)}) async-start(), calls=%async_computation.8 | async-start | bytes 16777216 | tf_op jit(solution)/shard_map/psum | solution.py:16
  330.6 5.8 copy-start
  330.6 99.0 %all-to-all-start = ((f32[4,32,128,128]{3,1,0,2:T(8,128)}), f32[4,32,128,128]{3,1,0,2:T(8,128)}, u32[]{:S(2)}, u32[]{:S(2)}) async-start(f32[4,32,128,128]{3,1,0,2:T(8,128)} %copy.28), calls=%async_computation | async-start | bytes 16777216 | tf_op jit(solution)/shard_map/all_to_all | solution.py:64
  363.5 71.7 %copy-start.3 = (f32[32,128,128]{2,1,0:T(8,128)S(1)}, f32[32,128,128]{2,1,0:T(8,128)}, u32[]{:S(2)}) copy-start(f32[32,128,128]{2,1,0:T(8,128)} %get-tuple-element.5) | copy-start | bytes 6291460
  429.5 98.9 %all-to-all-start.2 = ((f32[4,32,128,128]{3,1,0,2:T(8,128)}), f32[4,32,128,128]{3,1,0,2:T(8,128)}, u32[]{:S(2)}, u32[]{:S(2)}) async-start(f32[4,32,128,128]{3,1,0,2:T(8,128)} %copy.36), calls=%async_computation.2 | async-start | bytes 16777216 | tf_op jit(solution)/shard_map/all_to_all | solution.py:64
  462.7 71.4 %copy-start.5 = (f32[32,128,128]{2,1,0:T(8,128)S(1)}, f32[32,128,128]{2,1,0:T(8,128)}, u32[]{:S(2)}) copy-start(f32[32,128,128]{2,1,0:T(8,128)} %get-tuple-element.8) | copy-start | bytes 6291460
  528.4 98.9 %all-to-all-start.4 = ((f32[4,32,128,128]{3,1,0,2:T(8,128)}), f32[4,32,128,128]{3,1,0,2:T(8,128)}, u32[]{:S(2)}, u32[]{:S(2)}) async-start(f32[4,32,128,128]{3,1,0,2:T(8,128)} %copy.43), calls=%async_computation.4 | async-start | bytes 16777216 | tf_op jit(solution)/shard_map/all_to_all | solution.py:64
  561.2 71.9 %copy-start.7 = (s32[128,32,128]{2,1,0:T(8,128)S(1)}, s32[128,32,128]{2,1,0:T(8,128)}, u32[]{:S(2)}) copy-start(s32[128,32,128]{2,1,0:T(8,128)} %param.7) | copy-start | bytes 6291460
  627.3 98.8 %all-to-all-start.6 = ((f32[4,32,128,128]{3,1,0,2:T(8,128)}), f32[4,32,128,128]{3,1,0,2:T(8,128)}, u32[]{:S(2)}, u32[]{:S(2)}) async-start(f32[4,32,128,128]{3,1,0,2:T(8,128)} %copy.50), calls=%async_computation.6 | async-start | bytes 16777216 | tf_op jit(solution)/shard_map/all_to_all | solution.py:64
  726.1 98.8 %all-to-all-start.1 = ((f32[4,128,32,128]{3,2,0,1:T(8,128)}), f32[4,128,32,128]{3,2,0,1:T(8,128)}, u32[]{:S(2)}, u32[]{:S(2)}) async-start(f32[4,128,32,128]{3,2,0,1:T(8,128)} %copy.33), calls=%async_computation.1 | async-start | bytes 16777216 | tf_op jit(solution)/shard_map/all_to_all | solution.py:67
  824.9 98.9 %all-to-all-start.3 = ((f32[4,128,32,128]{3,2,0,1:T(8,128)}), f32[4,128,32,128]{3,2,0,1:T(8,128)}, u32[]{:S(2)}, u32[]{:S(2)}) async-start(f32[4,128,32,128]{3,2,0,1:T(8,128)} %copy.40), calls=%async_computation.3 | async-start | bytes 16777216 | tf_op jit(solution)/shard_map/all_to_all | solution.py:67
  923.8 98.8 %all-to-all-start.5 = ((f32[4,128,32,128]{3,2,0,1:T(8,128)}), f32[4,128,32,128]{3,2,0,1:T(8,128)}, u32[]{:S(2)}, u32[]{:S(2)}) async-start(f32[4,128,32,128]{3,2,0,1:T(8,128)} %copy.47), calls=%async_computation.5 | async-start | bytes 16777216 | tf_op jit(solution)/shard_map/all_to_all | solution.py:67
  969.6 58.8 %copy-start.4 = (f32[32,128,128]{2,1,0:T(8,128)S(1)}, f32[32,128,128]{2,1,0:T(8,128)}, u32[]{:S(2)}) copy-start(f32[32,128,128]{2,1,0:T(8,128)} %get-tuple-element.5) | copy-start | bytes 6291460
  1022.5 99.0 %all-to-all-start.7 = ((f32[4,128,32,128]{3,2,0,1:T(8,128)}), f32[4,128,32,128]{3,2,0,1:T(8,128)}, u32[]{:S(2)}, u32[]{:S(2)}) async-start(f32[4,128,32,128]{3,2,0,1:T(8,128)} %copy.54), calls=%async_computation.7 | async-start | bytes 16777216 | tf_op jit(solution)/shard_map/all_to_all | solution.py:67
  1028.4 4.1 copy-start.1
  1028.4 4.1 copy-start.2
  1125.9 9.4 copy-start.6
Sparse Core Ops, SparseCore 0:
  27.3 275.2 all-reduce.2
where the time goes:
time: 1170 us; the launch traced here: 1160 us
  waiting for transfers between devices  695 us (59%)
  matrix products  253 us (22%)
  local copies, waits for them, and re-layouts  132 us (11%)
  starting transfers between devices  46 us (4%)
  between operations  24.4 us (2%)
  other arithmetic  14.7 us (1%)
    psum x1, waiting for transfers between devices, broadcast(): return lax.psum(kept, axis)  275 us
    all_to_all x4, waiting for transfers between devices, per_device(): lax.all_to_all(spectrum, 'slab', split_axis=2, concat_axis=1, tiled=True)  249 us
    all_to_all x4, waiting for transfers between devices, per_device(): lax.all_to_all(potential, 'slab', split_axis=1, concat_axis=2, tiled=True)  170 us
    dot_general x8, matrix products, transform_first(): jnp.einsum('oxyz,kx->okyz', field, cas_rows, precision=lax.Precision.HIGH...  88.1 us
    dot_general x8, matrix products, transform_planes(): return jnp.einsum('oxyz,ky->oxkz', field, cas_rows, precision=highest)  87.7 us
    dot_general x8, matrix products, transform_planes(): field = jnp.einsum('oxyz,kz->oxyk', field, cas_rows, precision=highest)  77.6 us
    all_to_all x4, local copies, waits for them, and re-layouts, per_device(): lax.all_to_all(spectrum, 'slab', split_axis=2, concat_axis=1, tiled=True)  39.5 us
    transpose x4, local copies, waits for them, and re-layouts, transform_planes(): return jnp.einsum('oxyz,ky->oxkz', field, cas_rows, precision=highest)  34 us
  transfers between devices with their start and end apart: 9, of which 9 were waited for; matrix products, arithmetic and copies ran while one was open for 28% of the time, Pallas kernels for 0%

commit v1 on v0

--- a/solution.py
+++ b/solution.py
@@ -1,8 +1,11 @@
+import functools
 import math
 
 import jax
 import jax.numpy as jnp
 from jax import lax
+from jax.experimental import pallas as pl
+from jax.experimental.pallas import tpu as pltpu
 from jax.sharding import PartitionSpec as P
 
 GRID = 128
@@ -70,9 +73,199 @@
     return accumulated
 
 
+def split_halves(value):
+    high = value.astype(jnp.bfloat16)
+    low = (value - high.astype(jnp.float32)).astype(jnp.bfloat16)
+    return high, low
+
+
+def split_table(cas):
+    high = lax.reduce_precision(cas, 8, 7)
+    return high.astype(jnp.bfloat16), (cas - high).astype(jnp.bfloat16)
+
+
+def right_table(cas):
+    high, low = split_table(cas)
+    upper = jnp.concatenate([high, low], axis=1)
+    lower = jnp.concatenate([high, jnp.zeros_like(low)], axis=1)
+    return jnp.concatenate([upper, lower], axis=0)
+
+
+def left_table(cas):
+    high, low = split_table(cas)
+    upper = jnp.concatenate([high, high], axis=1)
+    lower = jnp.concatenate([low, jnp.zeros_like(low)], axis=1)
+    return jnp.concatenate([upper, lower], axis=0)
+
+
+def apply_right(rows, table):
+    high, low = split_halves(rows)
+    out = jnp.dot(jnp.concatenate([high, low], axis=1), table, preferred_element_type=jnp.float32)
+    return out[:, :GRID] + out[:, GRID:]
+
+
+def apply_left(table, pair):
+    high, low = split_halves(pair)
+    out = jnp.dot(table, jnp.concatenate([high, low], axis=0), preferred_element_type=jnp.float32)
+    return out[:GRID] + out[GRID:]
+
+
+STEPS = 8
+PLANES = GRID // STEPS
+
+
+def source_kernel(first, *refs):
+    if first:
+        target, source, coulomb, zt, yt, xt, yi, xi, out, field = refs
+        prior = None
+    else:
+        target, source, coulomb, zt, yt, xt, yi, xi, prior, out, field = refs
+    step = pl.program_id(0)
+
+    @pl.when(step < STEPS)
+    def _():
+        def pair(p, carry):
+            base = pl.multiple_of(p * 2 * GRID, 2 * GRID)
+            rows = target[pl.ds(base, 2 * GRID), :] * source[pl.ds(base, 2 * GRID), :]
+            rows = apply_right(rows, zt[...])
+            both = jnp.concatenate([rows[:GRID], rows[GRID:]], axis=1)
+            both = apply_left(yt[...], both)
+            plane = step * PLANES + p * 2
+            field[pl.ds(plane, GRID, stride=GRID), :] = both[:, :GRID]
+            field[pl.ds(plane + 1, GRID, stride=GRID), :] = both[:, GRID:]
+            return carry
+
+        lax.fori_loop(0, PLANES // 2, pair, 0, unroll=True)
+
+    @pl.when((step >= STEPS) & (step < 2 * STEPS))
+    def _():
+        def pair(p, carry):
+            base = pl.multiple_of(((step - STEPS) * PLANES + p * 2) * GRID, 2 * GRID)
+            local = pl.multiple_of(p * 2 * GRID, 2 * GRID)
+            both = jnp.concatenate([field[pl.ds(base, GRID), :], field[pl.ds(base + GRID, GRID), :]], axis=1)
+            weight = jnp.concatenate([coulomb[pl.ds(local, GRID), :], coulomb[pl.ds(local + GRID, GRID), :]], axis=1)
+            both = apply_left(xt[...], both) * weight
+            both = apply_left(xi[...], both)
+            field[pl.ds(base, GRID), :] = both[:, :GRID]
+            field[pl.ds(base + GRID, GRID), :] = both[:, GRID:]
+            return carry
+
+        lax.fori_loop(0, PLANES // 2, pair, 0, unroll=True)
+
+    @pl.when(step >= 2 * STEPS)
+    def _():
+        def pair(p, carry):
+            plane = (step - 2 * STEPS) * PLANES + p * 2
+            base = pl.multiple_of(p * 2 * GRID, 2 * GRID)
+            both = jnp.concatenate(
+                [field[pl.ds(plane, GRID, stride=GRID), :], field[pl.ds(plane + 1, GRID, stride=GRID), :]], axis=1
+            )
+            both = apply_left(yi[...], both)
+            rows = jnp.concatenate([both[:, :GRID], both[:, GRID:]], axis=0)
+            rows = apply_right(rows, zt[...]) * source[pl.ds(base, 2 * GRID), :]
+            if not first:
+                rows = rows + prior[pl.ds(base, 2 * GRID), :]
+            out[pl.ds(base, 2 * GRID), :] = rows
+            return carry
+
+        lax.fori_loop(0, PLANES // 2, pair, 0, unroll=True)
+
+
+def add_source(target, source, coulomb, tables, prior):
+    rows = PLANES * GRID
+    block = lambda index: pl.BlockSpec((rows, GRID), index)
+    whole = pl.BlockSpec((2 * GRID, 2 * GRID), lambda i: (0, 0))
+    last = STEPS - 1
+    begin = lambda i: (jnp.minimum(i, last), 0)
+    middle = lambda i: (jnp.clip(i - STEPS, 0, last), 0)
+    end = lambda i: (jnp.maximum(i - 2 * STEPS, 0), 0)
+    ends = lambda i: (jnp.where(i < 2 * STEPS, jnp.minimum(i, last), i - 2 * STEPS), 0)
+    first = prior is None
+    specs = [block(begin), block(ends), block(middle)] + [whole] * 5
+    operands = [target, source, coulomb] + list(tables)
+    if not first:
+        specs.append(block(end))
+        operands.append(prior)
+    cells = GRID * GRID
+    return pl.pallas_call(
+        functools.partial(source_kernel, first),
+        grid=(3 * STEPS,),
+        in_specs=specs,
+        out_specs=block(end),
+        out_shape=jax.ShapeDtypeStruct((cells, GRID), jnp.float32),
+        scratch_shapes=[pltpu.VMEM((cells, GRID), jnp.float32)],
+        compiler_params=pltpu.CompilerParams(vmem_limit_bytes=48 * 1024 * 1024),
+        cost_estimate=pl.CostEstimate(
+            flops=6 * 2 * 4 * cells * GRID * GRID, bytes_accessed=5 * 4 * cells * GRID, transcendentals=0
+        ),
+    )(*operands)
+
+
+def swap_slab(value, bits):
+    return lax.ppermute(value, "slab", [(s, s ^ bits) for s in range(4)])
+
+
+GROUP = 2
+
+
+def per_device_whole(orbitals, owner_band, owner_slot, g_mask):
+    band, slab = lax.axis_index("band"), lax.axis_index("slab")
+    depth = orbitals.shape[1]
+    cas = cas_matrix(GRID)
+    order = jnp.arange(GRID, dtype=jnp.int32)
+    order = ((order // depth) ^ slab) * depth + order % depth
+    cas_order = cas[order]
+    yt, yi = left_table(cas_order), left_table(cas_order.T)
+    tables = (right_table(cas), yt, yi, yi, yt)
+
+    targets = [lax.dynamic_index_in_dim(orbitals, slab ^ r, 0, keepdims=False) for r in range(4)]
+    targets = [targets[0]] + [swap_slab(targets[r], r) for r in (1, 2, 3)]
+    target = jnp.concatenate(targets, axis=0).reshape(GRID * GRID, GRID)
+
+    full_index = jnp.arange(GRID, dtype=jnp.int32)
+    column_index = slab * depth + jnp.arange(depth, dtype=jnp.int32)
+    first_sq = fold_index(full_index) ** 2
+    second_sq = fold_index(column_index) ** 2
+    squares = first_sq[:, None, None] + second_sq[None, :, None] + first_sq[None, None, :]
+    gain = -coulomb_gain / (GRID * GRID * GRID)
+    weight = (g_mask.astype(jnp.float32) * gain / (squares + 1.0)).transpose(1, 0, 2)
+    over = swap_slab(weight, 2)
+    near = jnp.concatenate([weight, swap_slab(weight, 1), over, swap_slab(over, 1)], axis=0)
+    coulomb = near.reshape(GRID * GRID, GRID)
+
+    result = None
+    count = owner_band.shape[0]
+    for start in range(0, count, GROUP):
+        mine = jnp.stack(
+            [
+                jnp.where(
+                    owner_band[which] == band,
+                    lax.dynamic_index_in_dim(orbitals, owner_slot[which], 0, keepdims=False),
+                    0.0,
+                )
+                for which in range(start, start + GROUP)
+            ]
+        )
+        spread = lax.psum(mine, "band")
+        for at in range(GROUP):
+            own = spread[at]
+            far = swap_slab(own, 2)
+            pieces = [own, swap_slab(own, 1), far, swap_slab(far, 1)]
+            source = jnp.concatenate(pieces, axis=0).reshape(GRID * GRID, GRID)
+            result = add_source(target, source, coulomb, tables, result)
+    result = result.reshape(4, depth, GRID, GRID)
+    parts = [result[0]] + [swap_slab(result[r], r) for r in (1, 2, 3)]
+    stacked = jnp.stack(parts, axis=0)
+    pairs = stacked.reshape(2, 2, depth, GRID, GRID)
+    pairs = jnp.where(slab % 2 == 1, pairs[:, ::-1], pairs)
+    pairs = jnp.where(slab // 2 == 1, pairs[::-1], pairs)
+    return pairs.reshape(orbitals.shape)
+
+
 def solution(mesh):
+    fits = mesh.shape["band"] == 8 and mesh.shape["slab"] == 4
     return jax.shard_map(
-        per_device,
+        per_device_whole if fits else per_device,
         mesh=mesh,
         in_specs=(P("band", "slab", None, None), P(), P(), P(None, "slab", None)),
         out_specs=P("band", "slab", None, None),

time: 1170 us -> 768 us (0.66)
  matrix products: 253 us -> 0 us
  waiting for transfers between devices: 695 us -> 504 us
  Pallas kernels: 0 us -> 141 us
  local copies, waits for them, and re-layouts: 132 us -> 24.5 us
  other arithmetic: 14.7 us -> 58.6 us
  starting transfers between devices: 46 us -> 13.8 us
    all_to_all x8 -> x0, waiting for transfers between devices: 419 us -> none  [the longest x4 249 us: per_device(): lax.all_to_all(spectrum, 'slab', split_axis=2, concat_axis=1, tiled=True)]
    dot_general x24 -> x0, matrix products: 253 us -> none  [the longest x8 88.1 us: transform_first(): jnp.einsum('oxyz,kx->okyz', field, cas_rows, precision=lax.Precision.HIGH...]
    ppermute x0 -> x21, waiting for transfers between devices: none -> 238 us  [swap_slab(): return lax.ppermute(value, 'slab', [(s, s ^ bits) for s in range(4)])]
    pallas_call x0 -> x4, Pallas kernels: none -> 141 us  [add_source(): pl.pallas_call(functools.partial(source_kernel, first), grid=(3 * STEPS,)...]
    transpose x8 -> x0, local copies, waits for them, and re-layouts: 66.7 us -> none  [the longest x4 34 us: transform_planes(): return jnp.einsum('oxyz,ky->oxkz', field, cas_rows, precision=highest)]
    all_to_all x8 -> x0, local copies, waits for them, and re-layouts: 60.9 us -> none  [the longest x4 39.5 us: per_device(): lax.all_to_all(spectrum, 'slab', split_axis=2, concat_axis=1, tiled=True)]
    all_to_all x8 -> x0, starting transfers between devices: 46 us -> none  [the longest x4 23.3 us: per_device(): lax.all_to_all(potential, 'slab', split_axis=1, concat_axis=2, tiled=True)]
    concatenate x0 -> x8, other arithmetic: none -> 32.8 us  [the longest x4 23.6 us: per_device_whole(): source = jnp.concatenate(pieces, axis=0).reshape(GRID * GRID, GRID)]
  transfers between devices with their start and end apart: 9 -> 22, of which waited for: 9 -> 8; matrix products, arithmetic and copies ran while one was open for 28% -> 6% of each run, Pallas kernels for 0% -> 14%
where the time goes in v1:
time: 768 us; the launch traced here: 765 us
  waiting for transfers between devices  504 us (66%)
  Pallas kernels  141 us (18%)
  other arithmetic  58.6 us (8%)
  local copies, waits for them, and re-layouts  24.5 us (3%)
  between operations  23.5 us (3%)
  starting transfers between devices  13.8 us (2%)
    psum x1, waiting for transfers between devices, per_device_whole(): spread = lax.psum(mine, 'band')  266 us
    ppermute x21, waiting for transfers between devices, swap_slab(): return lax.ppermute(value, 'slab', [(s, s ^ bits) for s in range(4)])  238 us
    pallas_call x4, Pallas kernels, add_source(): pl.pallas_call(functools.partial(source_kernel, first), grid=(3 * STEPS,)...  141 us
    concatenate x4, other arithmetic, per_device_whole(): source = jnp.concatenate(pieces, axis=0).reshape(GRID * GRID, GRID)  23.6 us
  transfers between devices with their start and end apart: 22, of which 8 were waited for; matrix products, arithmetic and copies ran while one was open for 6% of the time, Pallas kernels for 14%

profile of v1, /device:TPU:0, one launch (start us, length us, event | category | flops | bytes accessed | tf_op | source)
XLA Modules:
  0.0 765.4 jit_solution(14530831143576684777)
XLA Ops:
  19.4 9.1 %dynamic-slice_select_fusion.1 = (f32[1,32,128,128]{3,2,1,0:T(8,128)S(1)}, f32[1,32,128,128]{3,2,1,0:T(8,128)S(1)}, f32[1,32,128,128]{3,2,1,0:T(8,128)S(1)}, f32...) fusion(f32[4,32,128,128]{3,2,1,0:T(8,128)} %param.4, ...), kind=kLoop, calls=%fused_computation.17 | loop fusion | flops 2097152 | bytes 33554468 | tf_op jit(solution)/shard_map/jit(_where)/select_n | solution.py:241
  28.5 4.0 pad_maximum_fusion.7
  40.8 265.7 %all-reduce.6.cloned.1.call-done = (f32[2,32,128,128]{3,2,1,0:T(8,128)}, f32[2,32,128,128]{3,2,1,0:T(8,128)}) async-done(((f32[2,32,128,128]{3,2,1,0:T(8,128)}, f32[2,32,128,128]{3,2,1,0:T(8,128)}), (f32[2,32,128,128]{3,2,1,0:T(8,128)}, f32[2,32,128,128]{3,2,1,0:T(8,128)})) %all-reduce.6.cloned.1.call-update) | async-done | bytes 8388624 | tf_op jit(solution)/shard_map/psum | solution.py:249
  306.6 4.1 slice_bitcast_fusion
  317.0 42.3 %collective-permute-done.16 = f32[32,128,128]{2,1,0:T(8,128)} collective-permute-done((f32[32,128,128]{2,1,0:T(8,128)S(1)}, f32[32,128,128]{2,1,0:T(8,128)}, u32[]{:S(2)}, u32[]{:S(2)}) %collective-permute-start.16) | collective-permute-done | bytes 2097184 | tf_op jit(solution)/shard_map/ppermute | solution.py:205
  361.3 42.9 %collective-permute-done.13 = f32[32,128,128]{2,1,0:T(8,128)} collective-permute-done((f32[32,128,128]{2,1,0:T(8,128)}, f32[32,128,128]{2,1,0:T(8,128)}, u32[]{:S(2)}, u32[]{:S(2)}) %collective-permute-start.13) | collective-permute-done | bytes 2097184 | tf_op jit(solution)/shard_map/ppermute | solution.py:205
  405.7 6.0 pad_maximum_fusion
  411.7 37.5 %collective-permute-done.10 = f32[32,128,128]{2,1,0:T(8,128)} collective-permute-done((f32[32,128,128]{2,1,0:T(8,128)}, f32[32,128,128]{2,1,0:T(8,128)}, u32[]{:S(2)}, u32[]{:S(2)}) %collective-permute-start.10) | collective-permute-done | bytes 2097184 | tf_op jit(solution)/shard_map/ppermute | solution.py:205
  449.7 3.2 pad_maximum_fusion.2
  453.0 8.1 %copy.5 = f32[128,128,128]{2,1,0:T(8,128)} copy(f32[128,128,128]{2,0,1:T(8,128)S(1)} %pad_maximum_fusion.2) | data formatting | bytes 16777216 | tf_op jit(solution)/shard_map/concatenate | solution.py:233
  461.1 6.4 pad_maximum_fusion.5
  467.6 25.4 %collective-permute-done.4 = f32[32,128,128]{2,1,0:T(8,128)} collective-permute-done((f32[32,128,128]{2,1,0:T(8,128)}, f32[32,128,128]{2,1,0:T(8,128)}, u32[]{:S(2)}, u32[]{:S(2)}) %collective-permute-start.4) | collective-permute-done | bytes 2097184 | tf_op jit(solution)/shard_map/ppermute | solution.py:205
  493.0 6.0 pad_maximum_fusion.4
  499.0 34.0 %shard_map.46.refs_8_ = f32[16384,128]{1,0:T(8,128)} custom-call(f32[16384,128]{1,0:T(8,128)} %bitcast.47, f32[16384,128]{1,0:T(8,128)} %bitcast.55, f32[16384,128]{1,0:T(8,128)} %bitcast.51, bf16[256,256]{1,0:T(8,128)(2,1)S(1)} %fusion.3.refs_3_, bf16[256,256]{1,0:T(8,128)(2,1)S(1)} %get-tuple-element.39.refs_4_.refs_7_, ...), custom_call_target="tpu_custom_call" | custom-call | flops 12884901888 | bytes 41943040 | tf_op jit(solution)/shard_map/pallas_call | solution.py:190
  533.0 5.5 pad_maximum_fusion.3
  538.5 35.6 %shard_map.47.refs_8_ = f32[16384,128]{1,0:T(8,128)} custom-call(f32[16384,128]{1,0:T(8,128)} %bitcast.48, f32[16384,128]{1,0:T(8,128)} %bitcast.56, f32[16384,128]{1,0:T(8,128)} %bitcast.52, bf16[256,256]{1,0:T(8,128)(2,1)S(1)} %fusion.3.refs_3_, bf16[256,256]{1,0:T(8,128)(2,1)S(1)} %get-tuple-element.39.refs_4_.refs_7_, ...), custom_call_target="tpu_custom_call" | custom-call | flops 12884901888 | bytes 41943040 | tf_op jit(solution)/shard_map/pallas_call | solution.py:190
  574.1 35.5 %shard_map.48.refs_8_ = f32[16384,128]{1,0:T(8,128)} custom-call(f32[16384,128]{1,0:T(8,128)} %bitcast.49, f32[16384,128]{1,0:T(8,128)} %bitcast.58, f32[16384,128]{1,0:T(8,128)} %bitcast.53, bf16[256,256]{1,0:T(8,128)(2,1)S(1)} %fusion.3.refs_3_, bf16[256,256]{1,0:T(8,128)(2,1)S(1)} %get-tuple-element.39.refs_4_.refs_7_, ...), custom_call_target="tpu_custom_call" | custom-call | flops 12884901888 | bytes 41943040 | tf_op jit(solution)/shard_map/pallas_call | solution.py:190
  609.6 5.7 pad_maximum_fusion.1
  615.3 35.6 %shard_map.49 = f32[16384,128]{1,0:T(8,128)} custom-call(f32[16384,128]{1,0:T(8,128)} %bitcast.50, f32[16384,128]{1,0:T(8,128)} %bitcast.57, f32[16384,128]{1,0:T(8,128)} %bitcast.54, bf16[256,256]{1,0:T(8,128)(2,1)S(1)} %fusion.3.refs_3_, bf16[256,256]{1,0:T(8,128)(2,1)S(1)} %get-tuple-element.39.refs_4_.refs_7_, ...), custom_call_target="tpu_custom_call" | custom-call | flops 12884901888 | bytes 41943040 | tf_op jit(solution)/shard_map/pallas_call | solution.py:190
  650.8 6.3 fusion.23
  661.8 44.7 %collective-permute-done.19 = f32[32,128,128]{2,1,0:T(8,128)} collective-permute-done((f32[32,128,128]{2,1,0:T(8,128)}, f32[32,128,128]{2,1,0:T(8,128)}, u32[]{:S(2)}, u32[]{:S(2)}) %collective-permute-start.19) | collective-permute-done | bytes 2097184 | tf_op jit(solution)/shard_map/ppermute | solution.py:205
  706.5 43.0 %collective-permute-done.20 = f32[32,128,128]{2,1,0:T(8,128)} collective-permute-done((f32[32,128,128]{2,1,0:T(8,128)}, f32[32,128,128]{2,1,0:T(8,128)}, u32[]{:S(2)}, u32[]{:S(2)}) %collective-permute-start.20) | collective-permute-done | bytes 2097184 | tf_op jit(solution)/shard_map/ppermute | solution.py:205
  749.5 3.1 pad_maximum_fusion.6
  754.3 4.3 reverse_select_fusion
  (70 shorter events, 27.8 us)
Async XLA Ops:
  6.5 300.0 %all-reduce.6.cloned.1.call-start = ((), (), s32[]{:S(2)}) async-start(), calls=%async_computation | async-start | bytes 16777216 | tf_op jit(solution)/shard_map/psum | solution.py:249
  32.5 278.2 %collective-permute-start = (f32[32,128,128]{2,1,0:T(8,128)}, f32[32,128,128]{2,1,0:T(8,128)}, u32[]{:S(2)}, u32[]{:S(2)}) collective-permute-start(f32[32,128,128]{2,1,0:T(8,128)} %get-tuple-element.16), channel_id=1, source_target_pairs={{0,1},{1,0},{2,3},{3,2},{4,5},{5,4},{6,7},{7,6},{8,9},{9,8},{10,11... | collective-permute-start | bytes 6291464 | tf_op jit(solution)/shard_map/ppermute | solution.py:205
  35.9 276.3 %collective-permute-start.7 = (f32[32,128,128]{2,0,1:T(8,128)}, f32[32,128,128]{2,0,1:T(8,128)}, u32[]{:S(2)}, u32[]{:S(2)}) collective-permute-start(f32[32,128,128]{2,0,1:T(8,128)} %divide_bitcast_fusion), channel_id=1, source_target_pairs={{0,2},{1,3},{2,0},{3,1},{4,6},{5,7},{6,4},{7,5},{8,10},{9,11},{10,... | collective-permute-start | bytes 6291464 | tf_op jit(solution)/shard_map/ppermute | solution.py:205
  38.7 273.5 %collective-permute-start.1 = (f32[32,128,128]{2,1,0:T(8,128)}, f32[32,128,128]{2,1,0:T(8,128)}, u32[]{:S(2)}, u32[]{:S(2)}) collective-permute-start(f32[32,128,128]{2,1,0:T(8,128)} %get-tuple-element.15), channel_id=1, source_target_pairs={{0,2},{1,3},{2,0},{3,1},{4,6},{5,7},{6,4},{7,5},{8,10},{9,11},{10,... | collective-permute-start | bytes 6291464 | tf_op jit(solution)/shard_map/ppermute | solution.py:205
  38.7 274.0 %collective-permute-start.2 = (f32[32,128,128]{2,1,0:T(8,128)}, f32[32,128,128]{2,1,0:T(8,128)}, u32[]{:S(2)}, u32[]{:S(2)}) collective-permute-start(f32[32,128,128]{2,1,0:T(8,128)} %get-tuple-element.14), channel_id=1, source_target_pairs={{0,3},{1,2},{2,1},{3,0},{4,7},{5,6},{6,5},{7,4},{8,11},{9,10},{10,... | collective-permute-start | bytes 6291464 | tf_op jit(solution)/shard_map/ppermute | solution.py:205
  40.2 275.3 %collective-permute-start.6 = (f32[32,128,128]{2,0,1:T(8,128)}, f32[32,128,128]{2,0,1:T(8,128)}, u32[]{:S(2)}, u32[]{:S(2)}) collective-permute-start(f32[32,128,128]{2,0,1:T(8,128)} %divide_bitcast_fusion), channel_id=1, source_target_pairs={{0,1},{1,0},{2,3},{3,2},{4,5},{5,4},{6,7},{7,6},{8,9},{9,8},{10,11... | collective-permute-start | bytes 6291464 | tf_op jit(solution)/shard_map/ppermute | solution.py:205
  310.7 48.6 %collective-permute-start.16 = (f32[32,128,128]{2,1,0:T(8,128)S(1)}, f32[32,128,128]{2,1,0:T(8,128)}, u32[]{:S(2)}, u32[]{:S(2)}) collective-permute-start(f32[32,128,128]{2,1,0:T(8,128)S(1)} %get-tuple-element.19), channel_id=1, source_target_pairs={{0,2},{1,3},{2,0},{3,1},{4,6},{5,7},{6,4},{7,5},{8,10},{9,11},{10,... | collective-permute-start | bytes 6291464 | tf_op jit(solution)/shard_map/ppermute | solution.py:205
  312.2 47.2 %collective-permute-start.8 = (f32[32,128,128]{2,0,1:T(8,128)}, f32[32,128,128]{2,0,1:T(8,128)S(1)}, u32[]{:S(2)}, u32[]{:S(2)}) collective-permute-start(f32[32,128,128]{2,0,1:T(8,128)} %collective-permute-done.7), channel_id=1, source_target_pairs={{0,1},{1,0},{2,3},{3,2},{4,5},{5,4},{6,7},{7,6},{8,9},{9,8},{10,11... | collective-permute-start | bytes 6291464 | tf_op jit(solution)/shard_map/ppermute | solution.py:205
  312.2 47.7 %collective-permute-start.15 = (f32[32,128,128]{2,1,0:T(8,128)S(1)}, f32[32,128,128]{2,1,0:T(8,128)S(1)}, u32[]{:S(2)}, u32[]{:S(2)}) collective-permute-start(f32[32,128,128]{2,1,0:T(8,128)S(1)} %get-tuple-element.19), channel_id=1, source_target_pairs={{0,1},{1,0},{2,3},{3,2},{4,5},{5,4},{6,7},{7,6},{8,9},{9,8},{10,11... | collective-permute-start | bytes 6291464 | tf_op jit(solution)/shard_map/ppermute | solution.py:205
  312.7 91.6 %collective-permute-start.13 = (f32[32,128,128]{2,1,0:T(8,128)}, f32[32,128,128]{2,1,0:T(8,128)}, u32[]{:S(2)}, u32[]{:S(2)}) collective-permute-start(f32[32,128,128]{2,1,0:T(8,128)} %get-tuple-element.20), channel_id=1, source_target_pairs={{0,2},{1,3},{2,0},{3,1},{4,6},{5,7},{6,4},{7,5},{8,10},{9,11},{10,... | collective-permute-start | bytes 6291464 | tf_op jit(solution)/shard_map/ppermute | solution.py:205
  315.6 133.6 %collective-permute-start.10 = (f32[32,128,128]{2,1,0:T(8,128)}, f32[32,128,128]{2,1,0:T(8,128)}, u32[]{:S(2)}, u32[]{:S(2)}) collective-permute-start(f32[32,128,128]{2,1,0:T(8,128)} %get-tuple-element.21), channel_id=1, source_target_pairs={{0,2},{1,3},{2,0},{3,1},{4,6},{5,7},{6,4},{7,5},{8,10},{9,11},{10,... | collective-permute-start | bytes 6291464 | tf_op jit(solution)/shard_map/ppermute | solution.py:205
  359.3 89.9 %collective-permute-start.17 = (f32[32,128,128]{2,1,0:T(8,128)}, f32[32,128,128]{2,1,0:T(8,128)}, u32[]{:S(2)}, u32[]{:S(2)}) collective-permute-start(f32[32,128,128]{2,1,0:T(8,128)} %collective-permute-done.16), channel_id=1, source_target_pairs={{0,1},{1,0},{2,3},{3,2},{4,5},{5,4},{6,7},{7,6},{8,9},{9,8},{10,11... | collective-permute-start | bytes 6291464 | tf_op jit(solution)/shard_map/ppermute | solution.py:205
  359.3 45.0 %copy-start.3 = (f32[32,128,128]{2,0,1:T(8,128)}, f32[32,128,128]{2,0,1:T(8,128)S(1)}, u32[]{:S(2)}) copy-start(f32[32,128,128]{2,0,1:T(8,128)S(1)} %collective-permute-done.8) | copy-start | bytes 6291460
  359.3 108.2 %collective-permute-start.12 = (f32[32,128,128]{2,1,0:T(8,128)}, f32[32,128,128]{2,1,0:T(8,128)}, u32[]{:S(2)}, u32[]{:S(2)}) collective-permute-start(f32[32,128,128]{2,1,0:T(8,128)} %get-tuple-element.20), channel_id=1, source_target_pairs={{0,1},{1,0},{2,3},{3,2},{4,5},{5,4},{6,7},{7,6},{8,9},{9,8},{10,11... | collective-permute-start | bytes 6291464 | tf_op jit(solution)/shard_map/ppermute | solution.py:205
  359.8 44.5 %copy-start.5 = (f32[32,128,128]{2,1,0:T(8,128)}, f32[32,128,128]{2,1,0:T(8,128)S(1)}, u32[]{:S(2)}) copy-start(f32[32,128,128]{2,1,0:T(8,128)S(1)} %collective-permute-done.15) | copy-start | bytes 6291460
  359.8 133.1 %collective-permute-start.4 = (f32[32,128,128]{2,1,0:T(8,128)}, f32[32,128,128]{2,1,0:T(8,128)}, u32[]{:S(2)}, u32[]{:S(2)}) collective-permute-start(f32[32,128,128]{2,1,0:T(8,128)} %get-tuple-element.22), channel_id=1, source_target_pairs={{0,2},{1,3},{2,0},{3,1},{4,6},{5,7},{6,4},{7,5},{8,10},{9,11},{10,... | collective-permute-start | bytes 6291464 | tf_op jit(solution)/shard_map/ppermute | solution.py:205
  404.3 88.7 %collective-permute-start.14 = (f32[32,128,128]{2,1,0:T(8,128)}, f32[32,128,128]{2,1,0:T(8,128)}, u32[]{:S(2)}, u32[]{:S(2)}) collective-permute-start(f32[32,128,128]{2,1,0:T(8,128)} %collective-permute-done.13), channel_id=1, source_target_pairs={{0,1},{1,0},{2,3},{3,2},{4,5},{5,4},{6,7},{7,6},{8,9},{9,8},{10,11... | collective-permute-start | bytes 6291464 | tf_op jit(solution)/shard_map/ppermute | solution.py:205
  449.2 83.8 %collective-permute-start.9 = (f32[32,128,128]{2,1,0:T(8,128)}, f32[32,128,128]{2,1,0:T(8,128)S(1)}, u32[]{:S(2)}, u32[]{:S(2)}) collective-permute-start(f32[32,128,128]{2,1,0:T(8,128)} %get-tuple-element.21), channel_id=1, source_target_pairs={{0,1},{1,0},{2,3},{3,2},{4,5},{5,4},{6,7},{7,6},{8,9},{9,8},{10,11... | collective-permute-start | bytes 6291464 | tf_op jit(solution)/shard_map/ppermute | solution.py:205
  449.2 83.8 %collective-permute-start.11 = (f32[32,128,128]{2,1,0:T(8,128)}, f32[32,128,128]{2,1,0:T(8,128)S(1)}, u32[]{:S(2)}, u32[]{:S(2)}) collective-permute-start(f32[32,128,128]{2,1,0:T(8,128)} %collective-permute-done.10), channel_id=1, source_target_pairs={{0,1},{1,0},{2,3},{3,2},{4,5},{5,4},{6,7},{7,6},{8,9},{9,8},{10,11... | collective-permute-start | bytes 6291464 | tf_op jit(solution)/shard_map/ppermute | solution.py:205
  467.6 142.0 %collective-permute-start.3 = (f32[32,128,128]{2,1,0:T(8,128)}, f32[32,128,128]{2,1,0:T(8,128)S(1)}, u32[]{:S(2)}, u32[]{:S(2)}) collective-permute-start(f32[32,128,128]{2,1,0:T(8,128)} %get-tuple-element.22), channel_id=1, source_target_pairs={{0,1},{1,0},{2,3},{3,2},{4,5},{5,4},{6,7},{7,6},{8,9},{9,8},{10,11... | collective-permute-start | bytes 6291464 | tf_op jit(solution)/shard_map/ppermute | solution.py:205
  493.0 116.7 %collective-permute-start.5 = (f32[32,128,128]{2,1,0:T(8,128)}, f32[32,128,128]{2,1,0:T(8,128)S(1)}, u32[]{:S(2)}, u32[]{:S(2)}) collective-permute-start(f32[32,128,128]{2,1,0:T(8,128)} %collective-permute-done.4), channel_id=1, source_target_pairs={{0,1},{1,0},{2,3},{3,2},{4,5},{5,4},{6,7},{7,6},{8,9},{9,8},{10,11... | collective-permute-start | bytes 6291464 | tf_op jit(solution)/shard_map/ppermute | solution.py:205
  657.2 4.6 collective-permute-start.18
  657.7 48.8 %collective-permute-start.19 = (f32[32,128,128]{2,1,0:T(8,128)}, f32[32,128,128]{2,1,0:T(8,128)}, u32[]{:S(2)}, u32[]{:S(2)}) collective-permute-start(f32[32,128,128]{2,1,0:T(8,128)} %bitcast.28), channel_id=1, source_target_pairs={{0,2},{1,3},{2,0},{3,1},{4,6},{5,7},{6,4},{7,5},{8,10},{9,11},{10,... | collective-permute-start | bytes 6291464 | tf_op jit(solution)/shard_map/ppermute | solution.py:205
  659.1 90.4 %collective-permute-start.20 = (f32[32,128,128]{2,1,0:T(8,128)}, f32[32,128,128]{2,1,0:T(8,128)}, u32[]{:S(2)}, u32[]{:S(2)}) collective-permute-start(f32[32,128,128]{2,1,0:T(8,128)} %bitcast.30), channel_id=1, source_target_pairs={{0,3},{1,2},{2,1},{3,0},{4,7},{5,6},{6,5},{7,4},{8,11},{9,10},{10,... | collective-permute-start | bytes 6291464 | tf_op jit(solution)/shard_map/ppermute | solution.py:205
  (5 other events, 71.9 us)
Sparse Core Ops, SparseCore 0:
  32.6 273.8 all-reduce.5
